TPU v7x, 256 devices: a whole 4x4x8 slice. The times are simulated.
256 devices in a mesh: layer: 4 (over y_hi, core), rows: 4 (over x), feat: 16 (over z, y_lo).
Axes of the slice: x: 4, y: 4 (y_hi: 2, y_lo: 2; y = y_hi * 2 + y_lo), z: 8, core: 2. Of those that a mesh axis runs over, the one named last changes fastest.
Arguments:
- resid: bfloat16 [4, 512, 2304], P('layer', 'rows'), may hold values from -6 to 6
- norm_gain: float32 [4, 2304], P('layer'), may hold values from 0.5 to 2
- gate_weight: bfloat16 [4, 9216, 2304], P('layer', ('rows', 'feat')), may hold values from -0.125 to 0.125
- up_weight: bfloat16 [4, 9216, 2304], P('layer', ('rows', 'feat')), may hold values from -0.125 to 0.125
- down_weight: bfloat16 [4, 9216, 2304], P('layer', ('rows', 'feat')), may hold values from -0.0625 to 0.0625
- enc_weight: bfloat16 [4, 2304, 32768], P('layer', None, ('rows', 'feat')), may hold values from -0.125 to 0.125
- enc_bias: float32 [4, 32768], P('layer', ('rows', 'feat')), may hold values from -3 to 3
- dec_weight: bfloat16 [10, 32768, 2304], P(None, ('rows', 'feat'), 'layer'), may hold values from -0.03125 to 0.03125
- dec_bias: float32 [4, 2304], P(None, 'layer'), may hold values from -3 to 3
Outputs:
- errors: bfloat16 [512, 4, 2304], P(('rows', 'feat'), None, 'layer')
- act_grad: bfloat16 [4, 512, 32768], P('layer', None, ('rows', 'feat'))
All inputs are finite; a program needn't handle non-finite values.
Results may differ from a plain program's by a relative error of at most 0.017.
Values may be sent and summed in bfloat16 or wider, within the bound.
A program may use at most 128 MiB of HBM per device.

v0:
```python
import jax
import jax.numpy as jnp
from jax import lax
from jax.sharding import PartitionSpec as P


def pair_index(source, target, layers):
    return source * layers - source * (source - 1) // 2 + target - source


def normalize(resid_rows, gain_row):
    as_float = resid_rows.astype(jnp.float32)
    inv_rms = lax.rsqrt(jnp.mean(as_float * as_float, axis=-1, keepdims=True) + 1e-06)
    return (as_float * inv_rms * gain_row).astype(jnp.bfloat16)


def contract_last(left, right):
    return lax.dot_general(
        left, right, (((1,), (1,)), ((), ())), preferred_element_type=jnp.float32
    )


def decode_rows(features_all, dec_weight, target, layers, row_count):
    running = jnp.zeros((row_count, dec_weight.shape[2]), jnp.float32)
    for source in range(target + 1):
        row_block = features_all[source]
        running = running + jnp.dot(
            row_block,
            dec_weight[pair_index(source, target, layers)],
            preferred_element_type=jnp.float32,
        )
    return running


def body(
    resid,
    norm_gain,
    gate_weight,
    up_weight,
    down_weight,
    enc_weight,
    enc_bias,
    dec_weight,
    dec_bias,
):
    layers = lax.axis_size("layer")
    keep_rows = (
        resid.shape[1] * lax.axis_size("rows") // (lax.axis_size("rows") * lax.axis_size("feat"))
    )
    normed = normalize(resid[0], norm_gain[0])
    whole = lax.all_gather(normed, "rows", axis=0, tiled=True)
    gate_proj = contract_last(whole, gate_weight[0])
    up_proj = contract_last(whole, up_weight[0])
    hidden = (jax.nn.gelu(gate_proj, approximate=True) * up_proj).astype(jnp.bfloat16)
    mlp_part = jnp.dot(hidden, down_weight[0], preferred_element_type=jnp.float32)
    pre_act = jnp.dot(whole, enc_weight[0], preferred_element_type=jnp.float32) + enc_bias[0]
    features = jnp.maximum(pre_act, 0.0).astype(jnp.bfloat16)
    features_all = lax.all_gather(features[None], "layer", axis=0, tiled=True)
    mlp_rows = None
    reduced = lax.psum_scatter(mlp_part, ("rows", "feat"), scatter_dimension=0, tiled=True)
    mlp_rows = lax.all_to_all(
        reduced[:, None, :].astype(jnp.bfloat16), "layer", split_axis=2, concat_axis=1, tiled=True
    ).astype(jnp.float32)

    def target_term(target, row_count):
        partial_value = decode_rows(features_all, dec_weight, target, layers, row_count)
        return partial_value

    pieces = []
    for target in range(layers):

        def term_one(first_row, row_count, target=target):
            return target_term(target, row_count)

        pieces.append(
            lax.psum_scatter(
                term_one(jnp.int32(0), lax.axis_size(("rows", "feat")) * keep_rows),
                ("rows", "feat"),
                scatter_dimension=0,
                tiled=True,
            )
        )
    summed = jnp.stack(pieces, 1)
    error_f32 = summed + dec_bias[None]
    error_f32 = error_f32 - mlp_rows
    errors = error_f32.astype(jnp.bfloat16)
    shard_rows = lax.all_gather(errors, ("rows", "feat"), axis=0, tiled=True)
    per_source = []
    for source in range(layers):
        running = jnp.zeros((shard_rows.shape[0], dec_weight.shape[1]), jnp.float32)
        for target in range(source, layers):
            running = running + contract_last(
                shard_rows[:, target, :], dec_weight[pair_index(source, target, layers)]
            )
        per_source.append(running)
    gradients = jnp.stack(per_source, 0)
    act_grad = lax.psum_scatter(
        gradients.astype(jnp.bfloat16), "layer", scatter_dimension=0, tiled=True
    )
    return (errors, act_grad)


def solution(mesh):
    in_specs = (
        P("layer", "rows", None),
        P("layer", None),
        P("layer", ("rows", "feat"), None),
        P("layer", ("rows", "feat"), None),
        P("layer", ("rows", "feat"), None),
        P("layer", None, ("rows", "feat")),
        P("layer", ("rows", "feat")),
        P(None, ("rows", "feat"), "layer"),
        P(None, "layer"),
    )
    out_specs = (P(("rows", "feat"), None, "layer"), P("layer", None, ("rows", "feat")))
    return jax.shard_map(body, mesh=mesh, in_specs=in_specs, out_specs=out_specs, check_vma=False)
```

profile of v0, /device:TPU:1, one launch (start us, length us, event | category | flops | bytes accessed | tf_op | source)
XLA Modules:
  0.0 1471.8 jit_solution(9936259430973415305)
XLA Ops:
  7.2 1.4 fusion.18
  9.4 2.1 fusion.20
  11.6 39.4 %all-gather.5.cloned.1.call-done = bf16[512,2304]{1,0:T(8,128)(2,1)} async-done(((bf16[128,2304]{1,0:T(8,128)(2,1)}), bf16[512,2304]{1,0:T(8,128)(2,1)}) %all-gather.5.cloned.1.call-update) | async-done | bytes 2359312 | tf_op jit(solution)/shard_map/all_gather | solution.py:51
  51.0 3.8 fusion.8
  54.9 29.8 %all-gather.9.cloned.1.call-done = bf16[2048,512]{1,0:T(8,128)(2,1)} async-done(((bf16[512,512]{1,0:T(8,128)(2,1)}), bf16[2048,512]{1,0:T(8,128)(2,1)}) %all-gather.9.cloned.1.call-update) | async-done | bytes 2097168 | tf_op jit(solution)/shard_map/all_gather | solution.py:58
  84.8 2.0 fusion.48
  86.7 2.0 fusion.55
  88.7 2.0 fusion.60
  90.7 2.7 fusion.63
  93.4 1.7 convolution_add_fusion.2
  95.7 1.7 convolution_add_fusion
  98.1 1.7 convolution_add_fusion.3
  99.7 1.7 convolution_add_fusion.5
  101.5 2.8 fusion.101
  104.3 5.7 fusion.22
  112.0 570.1 %all-reduce.7.cloned.1.call-done = (f32[512,576]{1,0:T(8,128)}, f32[512,576]{1,0:T(8,128)}, f32[512,576]{1,0:T(8,128)}, f32[512,576]{1,0:T(8,128)}) async-done(((f32[512,576]{1,0:T(8,128)}, f32[512,576]{1,0:T(8,128)}, f32[512,576]{1,0:T(8,128)}, f32[512,576]{1,0:T(8,128)}), (f32[512,576]{1,0:T(8,128)}, f32[512,576]{1,0:T(8,128)}, f32[512,576]{1,0:T(8,128)}, ...) | async-done | bytes 4718608
  682.1 1.4 constant_dynamic-slice_fusion
  683.5 316.0 %reduce-scatter.3.cloned.1.call-done = f32[8,2304]{1,0:T(8,128)} async-done(((f32[512,2304]{1,0:T(8,128)}), f32[8,2304]{1,0:T(8,128)}) %reduce-scatter.3.cloned.1.call-update) | async-done | bytes 73744 | tf_op jit(solution)/shard_map/reduce_scatter | solution.py:60
  999.5 1.5 convert_bitcast_fusion
  1001.0 2.6 copy.28
  1004.1 13.7 reduce.1
  1017.8 2.3 reshape.37
  1020.1 53.2 %all-to-all-start = ((bf16[4,2,2304]{2,1,0:T(2,128)(2,1)}), bf16[4,2,2304]{2,1,0:T(2,128)(2,1)}, u32[]{:S(2)}, u32[]{:S(2)}) async-start(bf16[4,2,2304]{2,1,0:T(2,128)(2,1)} %reshape.37), calls=%async_computation.1 | async-start | bytes 73728 | tf_op jit(solution)/shard_map/all_to_all | solution.py:61
  1073.3 0.7 constant_dynamic-slice_fusion.2
  1074.0 1.3 stack.38
  1075.3 1.3 stack.37
  1078.0 2.5 reshape.38
  1080.6 2.1 copy.29
  1082.7 0.9 reshape.22
  1083.6 1.5 fusion.105
  1085.2 251.5 %all-gather.7.cloned.1.call-done = bf16[512,4,576]{2,1,0:T(4,128)(2,1)} async-done(((bf16[8,4,576]{2,1,0:T(4,128)(2,1)}), bf16[512,4,576]{2,1,0:T(4,128)(2,1)}) %all-gather.7.cloned.1.call-update) | async-done | bytes 2359312 | tf_op jit(solution)/shard_map/all_gather | solution.py:87
  1336.6 10.4 fusion.106
  1347.0 2.5 copy.37
  1349.5 2.5 fusion.17
  1352.0 2.5 copy.36
  1354.5 1.7 fusion.32
  1356.2 2.5 fusion.14
  1358.6 3.6 copy.35
  1362.2 1.8 fusion.36
  1364.1 1.7 convolution_add_fusion.8
  1365.7 2.5 fusion.15
  1368.2 3.6 copy.34
  1371.8 1.9 fusion.39
  1373.8 1.7 convolution_add_fusion.11
  1375.4 1.7 convolution_add_fusion.10
  1377.1 1.8 fusion.16
  1378.9 1.6 pad_maximum_fusion
  1380.6 84.4 %reduce-scatter.5.cloned.1.call-done = bf16[1,512,512]{2,1,0:T(8,128)(2,1)} async-done(((bf16[4,512,512]{2,1,0:T(8,128)(2,1)}), bf16[1,512,512]{2,1,0:T(8,128)(2,1)}) %reduce-scatter.5.cloned.1.call-update) | async-done | bytes 524304 | tf_op jit(solution)/shard_map/reduce_scatter | solution.py:97
  (46 shorter events, 5.4 us)
Async XLA Ops:
  7.2 43.8 %copy-start = (bf16[1,2304,512]{2,1,0:T(8,128)(2,1)S(1)}, bf16[1,2304,512]{2,1,0:T(8,128)(2,1)}, u32[]{:S(2)}) copy-start(bf16[1,2304,512]{2,1,0:T(8,128)(2,1)} %param.14) | copy-start | bytes 7077892
  7.2 43.8 %copy-start.8 = (f32[1,512]{1,0:T(1,128)S(1)}, f32[1,512]{1,0:T(1,128)}, u32[]{:S(2)}) copy-start(f32[1,512]{1,0:T(1,128)} %param.15) | copy-start | bytes 6148
  7.2 43.8 %all-gather.5.cloned.1.call-start = ((), (), s32[]{:S(2)}) async-start(), calls=%async_computation.3 | async-start | bytes 2949120 | tf_op jit(solution)/shard_map/all_gather | solution.py:51
  11.5 73.2 %all-gather.9.cloned.1.call-start = ((), (), s32[]{:S(2)}) async-start(), calls=%async_computation.7 | async-start | bytes 2621440 | tf_op jit(solution)/shard_map/all_gather | solution.py:58
  54.9 627.2 %all-reduce.7.cloned.1.call-start = ((), (), s32[]{:S(2)}) async-start(), calls=%async_computation.8 | async-start | bytes 10485760
  84.8 10.3 slice-start
  86.7 4.0 copy-start.1
  88.7 6.4 slice-start.1
  101.4 2.9 copy-start.5
  101.5 898.0 %reduce-scatter.3.cloned.1.call-start = ((), (), s32[]{:S(2)}) async-start(), calls=%async_computation.4 | async-start | bytes 4792320 | tf_op jit(solution)/shard_map/reduce_scatter | solution.py:60
  110.0 0.7 copy-start.9
  1017.8 65.8 %copy-start.7 = (f32[4,576]{1,0:T(4,128)S(1)}, f32[4,576]{1,0:T(4,128)}, u32[]{:S(2)}) copy-start(f32[4,576]{1,0:T(4,128)} %param.17) | copy-start | bytes 27652
  1020.1 58.0 %all-to-all-start = ((bf16[4,2,2304]{2,1,0:T(2,128)(2,1)}), bf16[4,2,2304]{2,1,0:T(2,128)(2,1)}, u32[]{:S(2)}, u32[]{:S(2)}) async-start(bf16[4,2,2304]{2,1,0:T(2,128)(2,1)} %reshape.37), calls=%async_computation.1 | async-start | bytes 73728 | tf_op jit(solution)/shard_map/all_to_all | solution.py:61
  1073.3 263.4 %all-gather.7.cloned.1.call-start = ((), (), s32[]{:S(2)}) async-start(), calls=%async_computation.5 | async-start | bytes 2662400 | tf_op jit(solution)/shard_map/all_gather | solution.py:87
  1085.1 379.9 %reduce-scatter.5.cloned.1.call-start = ((), (), s32[]{:S(2)}) async-start(), calls=%async_computation.6 | async-start | bytes 2621440 | tf_op jit(solution)/shard_map/reduce_scatter | solution.py:97
  1371.8 1.9 copy-start.2
  1377.1 1.8 copy-start.3
  1377.1 1.8 copy-start.4
  1377.1 1.8 copy-start.6
Sparse Core Ops, SparseCore 0:
  11.6 39.3 all-gather.4
  55.0 29.7 all-gather.8
  101.6 580.4 all-reduce.6
  684.5 314.9 reduce-scatter.2
  1085.2 251.3 all-gather.6
  1380.7 84.2 reduce-scatter.4
where the time goes:
time: 1470 us
  waiting for transfers between devices  1290 us (88%)
  starting transfers between devices  53.4 us (4%)
  matrix products  48.5 us (3%)
  local copies, waits for them, and re-layouts  40.8 us (3%)
  other arithmetic  22.6 us (2%)
  between operations  15 us (1%)
    unnamed x7, waiting for transfers between devices  570 us
    reduce_scatter x1, waiting for transfers between devices, body(): lax.psum_scatter(mlp_part, ('rows', 'feat'), scatter_dimension=0, tiled=T...  316 us
    all_gather x1, waiting for transfers between devices, body(): shard_rows = lax.all_gather(errors, ('rows', 'feat'), axis=0, tiled=True)  251 us
    reduce_scatter x1, waiting for transfers between devices, body(): lax.psum_scatter(gradients.astype(jnp.bfloat16), 'layer', scatter_dimensi...  84.4 us
    all_to_all x1, starting transfers between devices, body(): lax.all_to_all(reduced[:, None, :].astype(jnp.bfloat16), 'layer', split_a...  53.2 us
    all_gather x1, waiting for transfers between devices, body(): whole = lax.all_gather(normed, 'rows', axis=0, tiled=True)  39.4 us
    all_gather x1, waiting for transfers between devices, body(): features_all = lax.all_gather(features[None], 'layer', axis=0, tiled=True)  29.8 us
  transfers between devices with their start and end apart: 7, of which 7 were waited for; matrix products, arithmetic and copies ran while one was open for 1% of the time, Pallas kernels for 0%

commit v1 on v0

--- a/solution.py
+++ b/solution.py
@@ -58,8 +58,16 @@
     features_all = lax.all_gather(features[None], "layer", axis=0, tiled=True)
     mlp_rows = None
     reduced = lax.psum_scatter(mlp_part, ("rows", "feat"), scatter_dimension=0, tiled=True)
-    mlp_rows = lax.all_to_all(
-        reduced[:, None, :].astype(jnp.bfloat16), "layer", split_axis=2, concat_axis=1, tiled=True
+    mlp_rows = jnp.concatenate(
+        lax.all_to_all(
+            jnp.stack(
+                jnp.split(reduced[:, None, :].astype(jnp.bfloat16), lax.axis_size("layer"), axis=2)
+            ),
+            "layer",
+            0,
+            0,
+        ),
+        axis=1,
     ).astype(jnp.float32)
 
     def target_term(target, row_count):

time: 1470 us -> 1410 us (0.959)
  local copies, waits for them, and re-layouts: 40.8 us -> 3.5 us
    unnamed x34 -> x26, local copies, waits for them, and re-layouts: 20.9 us -> 1.93 us
where the time goes in v1:
time: 1410 us
  waiting for transfers between devices  1290 us (91%)
  starting transfers between devices  55 us (4%)
  matrix products  41 us (3%)
  between operations  15 us (1%)
    unnamed x7, waiting for transfers between devices  570 us
    reduce_scatter x1, waiting for transfers between devices, body(): lax.psum_scatter(mlp_part, ('rows', 'feat'), scatter_dimension=0, tiled=T...  315 us
    all_gather x1, waiting for transfers between devices, body(): shard_rows = lax.all_gather(errors, ('rows', 'feat'), axis=0, tiled=True)  249 us
    reduce_scatter x1, waiting for transfers between devices, body(): lax.psum_scatter(gradients.astype(jnp.bfloat16), 'layer', scatter_dimensi...  83.9 us
    all_to_all x1, starting transfers between devices, body(): lax.all_to_all(jnp.stack(jnp.split(reduced[:, None, :].astype(jnp.bfloat1...  54.8 us
    all_gather x1, waiting for transfers between devices, body(): whole = lax.all_gather(normed, 'rows', axis=0, tiled=True)  39.4 us
    all_gather x1, waiting for transfers between devices, body(): features_all = lax.all_gather(features[None], 'layer', axis=0, tiled=True)  29.8 us
  transfers between devices with their start and end apart: 7, of which 7 were waited for; matrix products, arithmetic and copies ran while one was open for 1% of the time, Pallas kernels for 0%

profile of v1, /device:TPU:1, one launch (start us, length us, event | category | flops | bytes accessed | tf_op | source)
XLA Modules:
  0.0 1414.1 jit_solution(14416404798691144975)
XLA Ops:
  7.2 1.4 fusion.18
  8.7 0.7 reduce
  9.4 2.1 fusion.20
  11.5 0.0 all-gather.9.cloned.1.call-start
  11.6 39.4 %all-gather.5.cloned.1.call-done = bf16[512,2304]{1,0:T(8,128)(2,1)} async-done(((bf16[128,2304]{1,0:T(8,128)(2,1)}), bf16[512,2304]{1,0:T(8,128)(2,1)}) %all-gather.5.cloned.1.call-update) | async-done | bytes 2359312 | tf_op jit(solution)/shard_map/all_gather | solution.py:51
  51.0 3.8 fusion.8
  54.9 0.0 all-reduce.7.cloned.1.call-start
  55.0 29.8 %all-gather.9.cloned.1.call-done = bf16[2048,512]{1,0:T(8,128)(2,1)} async-done(((bf16[512,512]{1,0:T(8,128)(2,1)}), bf16[2048,512]{1,0:T(8,128)(2,1)}) %all-gather.9.cloned.1.call-update) | async-done | bytes 2097168 | tf_op jit(solution)/shard_map/all_gather | solution.py:58
  84.8 2.0 fusion.36
  86.8 2.0 fusion.44
  88.8 1.9 fusion.50
  90.7 2.7 fusion.53
  93.5 1.7 convolution_add_fusion.2
  95.2 0.6 convolution_add_fusion.1
  95.8 1.7 convolution_add_fusion
  97.5 0.6 convolution_add_fusion.4
  98.1 1.7 convolution_add_fusion.3
  99.8 1.7 convolution_add_fusion.5
  101.5 0.0 reduce-scatter.3.cloned.1.call-start
  101.6 2.8 fusion.91
  104.4 5.7 fusion.22
  110.2 0.6 copy-done.7
  110.8 0.6 dynamic-slice
  112.1 570.0 %all-reduce.7.cloned.1.call-done = (f32[512,576]{1,0:T(8,128)}, f32[512,576]{1,0:T(8,128)}, f32[512,576]{1,0:T(8,128)}, f32[512,576]{1,0:T(8,128)}) async-done(((f32[512,576]{1,0:T(8,128)}, f32[512,576]{1,0:T(8,128)}, f32[512,576]{1,0:T(8,128)}, f32[512,576]{1,0:T(8,128)}), (f32[512,576]{1,0:T(8,128)}, f32[512,576]{1,0:T(8,128)}, f32[512,576]{1,0:T(8,128)}, ...) | async-done | bytes 4718608
  682.0 0.7 dynamic-slice_bitcast_fusion.2
  682.8 315.5 %reduce-scatter.3.cloned.1.call-done = f32[8,2304]{1,0:T(8,128)} async-done(((f32[512,2304]{1,0:T(8,128)}), f32[8,2304]{1,0:T(8,128)}) %reduce-scatter.3.cloned.1.call-update) | async-done | bytes 73744 | tf_op jit(solution)/shard_map/reduce_scatter | solution.py:60
  998.2 0.9 convert_bitcast_fusion
  999.1 0.1 slice_bitcast_fusion.17
  999.2 0.6 pad_maximum_fusion.1
  999.8 54.8 %all-to-all-start = ((bf16[4,8,1,576]{3,1,2,0:T(8,128)(2,1)}), bf16[4,8,1,576]{3,1,2,0:T(8,128)(2,1)S(1)}, u32[]{:S(2)}, u32[]{:S(2)}) async-start(bf16[4,8,1,576]{3,1,2,0:T(8,128)(2,1)} %pad_maximum_fusion.1), calls=%async_computation.1 | async-start | bytes 81920 | tf_op jit(solution)/shard_map/all_to_all | solution.py:62
  1054.6 0.7 dynamic-slice_bitcast_fusion
  1055.4 3.9 all-to-all-done
  1059.3 0.6 fusion.95
  1060.0 0.0 reduce-scatter.5.cloned.1.call-start
  1060.0 248.9 %all-gather.7.cloned.1.call-done = bf16[512,4,576]{2,0,1:T(8,128)(2,1)} async-done(((bf16[8,4,576]{2,0,1:T(8,128)(2,1)}), bf16[512,4,576]{2,0,1:T(8,128)(2,1)}) %all-gather.7.cloned.1.call-update) | async-done | bytes 2359312 | tf_op jit(solution)/shard_map/all_gather | solution.py:95
  1308.9 2.0 fusion.28
  1310.9 2.0 fusion.46
  1312.9 2.0 fusion.38
  1314.9 1.6 fusion.17
  1316.6 1.6 convolution_add_fusion.11
  1318.2 0.6 convolution_add_fusion.10
  1318.8 0.6 fusion.16
  1319.4 0.6 convolution_add_fusion.8
  1320.0 0.6 fusion.15
  1320.5 0.6 fusion.14
  1321.1 1.6 pad_maximum_fusion
  1322.7 0.6 copy.16
  1323.4 83.9 %reduce-scatter.5.cloned.1.call-done = bf16[1,512,512]{2,1,0:T(8,128)(2,1)} async-done(((bf16[4,512,512]{2,1,0:T(8,128)(2,1)}), bf16[1,512,512]{2,1,0:T(8,128)(2,1)}) %reduce-scatter.5.cloned.1.call-update) | async-done | bytes 524304 | tf_op jit(solution)/shard_map/reduce_scatter | solution.py:105
  (34 shorter events, 0.2 us)
Async XLA Ops:
  7.2 43.9 %copy-start = (bf16[1,2304,512]{2,1,0:T(8,128)(2,1)S(1)}, bf16[1,2304,512]{2,1,0:T(8,128)(2,1)}, u32[]{:S(2)}) copy-start(bf16[1,2304,512]{2,1,0:T(8,128)(2,1)} %param.14) | copy-start | bytes 7077892
  7.2 43.9 %copy-start.6 = (f32[1,512]{1,0:T(1,128)S(1)}, f32[1,512]{1,0:T(1,128)}, u32[]{:S(2)}) copy-start(f32[1,512]{1,0:T(1,128)} %param.15) | copy-start | bytes 6148
  7.2 43.9 %all-gather.5.cloned.1.call-start = ((), (), s32[]{:S(2)}) async-start(), calls=%async_computation.3 | async-start | bytes 2949120 | tf_op jit(solution)/shard_map/all_gather | solution.py:51
  11.5 73.2 %all-gather.9.cloned.1.call-start = ((), (), s32[]{:S(2)}) async-start(), calls=%async_computation.7 | async-start | bytes 2621440 | tf_op jit(solution)/shard_map/all_gather | solution.py:58
  54.9 627.1 %all-reduce.7.cloned.1.call-start = ((), (), s32[]{:S(2)}) async-start(), calls=%async_computation.8 | async-start | bytes 10485760
  84.8 10.4 slice-start
  86.8 4.0 copy-start.1
  88.7 6.4 slice-start.1
  101.5 2.9 copy-start.3
  101.5 896.7 %reduce-scatter.3.cloned.1.call-start = ((), (), s32[]{:S(2)}) async-start(), calls=%async_computation.4 | async-start | bytes 4792320 | tf_op jit(solution)/shard_map/reduce_scatter | solution.py:60
  110.1 0.7 copy-start.7
  110.1 949.2 %copy-start.5 = (f32[4,576]{1,0:T(4,128)S(1)}, f32[4,576]{1,0:T(4,128)}, u32[]{:S(2)}) copy-start(f32[4,576]{1,0:T(4,128)} %param.17) | copy-start | bytes 27652
  999.8 59.5 %all-to-all-start = ((bf16[4,8,1,576]{3,1,2,0:T(8,128)(2,1)}), bf16[4,8,1,576]{3,1,2,0:T(8,128)(2,1)S(1)}, u32[]{:S(2)}, u32[]{:S(2)}) async-start(bf16[4,8,1,576]{3,1,2,0:T(8,128)(2,1)} %pad_maximum_fusion.1), calls=%async_computation.1 | async-start | bytes 81920 | tf_op jit(solution)/shard_map/all_to_all | solution.py:62
  1054.6 254.3 %all-gather.7.cloned.1.call-start = ((), (), s32[]{:S(2)}) async-start(), calls=%async_computation.5 | async-start | bytes 2662400 | tf_op jit(solution)/shard_map/all_gather | solution.py:95
  1060.0 347.3 %reduce-scatter.5.cloned.1.call-start = ((), (), s32[]{:S(2)}) async-start(), calls=%async_computation.6 | async-start | bytes 2621440 | tf_op jit(solution)/shard_map/reduce_scatter | solution.py:105
  1308.9 9.3 slice-start.2
  1310.9 4.0 copy-start.2
  1312.9 5.3 slice-start.3
  1321.1 1.6 copy-start.4
Sparse Core Ops, SparseCore 0:
  11.7 39.3 all-gather.4
  55.0 29.7 all-gather.8
  101.6 580.3 all-reduce.6
  684.4 313.7 reduce-scatter.2
  1060.1 248.7 all-gather.6
  1322.9 84.3 reduce-scatter.4
